TPU v7x, 32 devices: a whole 2x2x4 slice. The times are simulated.
32 devices in a mesh: groups: 2 (over y), store: 4 (over x, core), tensor: 4 (over z).
Axes of the slice: x: 2, y: 2, z: 4, core: 2. Of those that a mesh axis runs over, the one named last changes fastest.
Arguments:
- hidden: bfloat16 [512, 8192], P(('groups', 'store', 'tensor')), parts along dimension 0, may hold values from -6 to 6
- queries: bfloat16 [512, 8192], P(('groups', 'store', 'tensor')), parts along dimension 0
- cached_key_rows: bfloat16 [512, 8, 128, 128], P(('groups', 'store', 'tensor')), parts along dimension 0
- cached_value_rows: bfloat16 [512, 8, 128, 128], P(('groups', 'store', 'tensor')), parts along dimension 0, may hold values from -6 to 6
- cache_length: int32 [512], P(('groups', 'store', 'tensor')), parts along dimension 0, may hold values from 2 to 128
- output_weight: bfloat16 [8192, 8192], P('tensor'), may hold values from -0.5 to 0.5
- shrink_matrices: bfloat16 [256, 64, 8192], P(('groups', 'store'), None, 'tensor'), parts along dimension 0, may hold values from -0.5 to 0.5
- expand_matrices: bfloat16 [256, 64, 8192], P(('groups', 'store'), 'tensor'), parts along dimension 0, may hold values from -0.75 to 0.75
- block_slot_rows: int32 [64, 16], P(('groups', 'store')), parts along dimension 0, may hold values from -1 to 63, as said below
- adapter_per_block: int32 [64], P(('groups', 'store')), parts along dimension 0, may hold values from 0 to 127, as said below
- adapter_store_slot: int32 [256], P('groups'), parts along dimension 0, may hold values from 0 to 127, as said below
Outputs:
- mixed: bfloat16 [512, 8192], P(('groups', 'store', 'tensor')), parts along dimension 0
There are 2 independent parts, one for each index of `groups`. A program takes and returns all parts, laid end to end along the dimension named above; an argument that names none is the same for every part. Nothing has to cross between parts.
Inputs may be any that keep to these rules, and one draw needn't show every extreme that they name: `block_slot_rows`: every row of a sub-group stands in exactly one slot of that sub-group's blocks; empty slots hold -1. `adapter_per_block`: in every sub-group, at most 4 blocks name an adapter whose slot lies with one store index (slot // 32), and some store index has exactly 4. `adapter_store_slot`: A permutation.
All inputs are finite; a program needn't handle non-finite values.
Results may differ from a plain program's by a relative error of at most 0.013.
Values may be sent and summed in bfloat16 or wider, within the bound.
A program may use at most 192 MiB of HBM per device.

v0:
```python
import jax
import jax.numpy as jnp
from jax import lax
from jax.sharding import PartitionSpec as P

ADAPTER_SCALE = 2.0


def attend(queries, cached_key_rows, cached_value_rows, cache_length):
    rows_dev, kv_heads, positions, head_dim = cached_key_rows.shape
    grouped = queries.reshape(rows_dev, kv_heads, -1, head_dim)
    scores = jnp.einsum(
        "rkgd,rkpd->rkgp", grouped, cached_key_rows, preferred_element_type=jnp.float32
    ) * head_dim ** (-0.5)
    live_pos = lax.broadcasted_iota(jnp.int32, (rows_dev, positions), 1) < cache_length[:, None]
    scores = jnp.where(live_pos[:, None, None, :], scores, -jnp.inf)
    highest = jnp.max(scores, axis=-1, keepdims=True)
    raised = jnp.exp(scores - highest)
    weights = (raised / jnp.sum(raised, axis=-1, keepdims=True)).astype(jnp.bfloat16)
    outputs = jnp.einsum(
        "rkgp,rkpd->rkgd", weights, cached_value_rows, preferred_element_type=jnp.float32
    )
    return outputs.astype(jnp.bfloat16).reshape(rows_dev, -1)


def place_in_owner(owner_ids, store_count):
    owner_hot = (owner_ids[..., None] == jnp.arange(store_count, dtype=jnp.int32)).astype(jnp.int32)
    return jnp.sum(jnp.cumsum(owner_hot, axis=-2) * owner_hot, axis=-1) - 1


def on_device(
    hidden,
    queries,
    cached_key_rows,
    cached_value_rows,
    cache_length,
    output_weight,
    shrink_matrices,
    expand_matrices,
    block_slot_rows,
    adapter_per_block,
    adapter_store_slot,
):
    attended = attend(queries, cached_key_rows, cached_value_rows, cache_length)
    head_rows = lax.all_to_all(attended, "tensor", split_axis=1, concat_axis=0, tiled=True)
    group_rows = head_rows.shape[0]
    slots_per_holder = shrink_matrices.shape[0]
    blocks_here = adapter_per_block.shape[0]
    capacity = blocks_here // 2
    store_count = lax.axis_size("store")
    rank_portion = expand_matrices.shape[1]
    slot_of = adapter_store_slot[adapter_per_block]
    requests = lax.all_gather(adapter_per_block, "store", axis=0, tiled=True)
    wanted = adapter_store_slot[requests].reshape(store_count, blocks_here)
    owner_all = wanted // slots_per_holder
    local_all = wanted % slots_per_holder
    position_all = place_in_owner(owner_all, store_count)
    store_index = lax.axis_index("store")
    chosen = (owner_all == store_index)[..., None] & (
        position_all[..., None] == jnp.arange(capacity, dtype=jnp.int32)
    )
    outgoing_local = jnp.sum(chosen.astype(jnp.int32) * local_all[..., None], axis=1)
    filled_rows = jnp.any(chosen, axis=1)
    empty_value = jnp.zeros((), jnp.bfloat16)
    outgoing_shrink = jnp.where(
        filled_rows[..., None, None], shrink_matrices[outgoing_local], empty_value
    )
    outgoing_expand = jnp.where(
        filled_rows[..., None, None], expand_matrices[outgoing_local], empty_value
    )
    recv_a, recv_b = (
        lax.all_to_all(outgoing_shrink, "store", split_axis=0, concat_axis=0, tiled=True),
        lax.all_to_all(outgoing_expand, "store", split_axis=0, concat_axis=0, tiled=True),
    )
    owner_mine = slot_of // slots_per_holder
    position_mine = place_in_owner(owner_mine, store_count)
    flat_place = owner_mine * capacity + position_mine
    fetched_a = recv_a.reshape((store_count * capacity,) + recv_a.shape[2:])[flat_place]
    fetched_b = recv_b.reshape((store_count * capacity,) + recv_b.shape[2:])[flat_place]
    live_slot = block_slot_rows >= 0
    picked = jnp.where(
        live_slot[..., None],
        head_rows[jnp.maximum(block_slot_rows, 0)],
        jnp.zeros((), jnp.bfloat16),
    )
    shrink_part = jnp.einsum("bsh,brh->bsr", picked, fetched_a, preferred_element_type=jnp.float32)
    summed_shrink = lax.psum(shrink_part, "tensor")
    shrink_output = lax.dynamic_slice_in_dim(
        summed_shrink, lax.axis_index("tensor") * rank_portion, rank_portion, 2
    )
    shrink_output = shrink_output.astype(jnp.bfloat16)
    targets = jnp.where(live_slot, block_slot_rows, group_rows)
    block_ids = lax.broadcasted_iota(jnp.int32, block_slot_rows.shape, 0)
    row_shrink = (
        jnp.zeros((group_rows + 1, blocks_here, rank_portion), jnp.bfloat16)
        .at[targets, block_ids]
        .set(shrink_output)
    )
    row_shrink = row_shrink[:group_rows].reshape(group_rows, blocks_here * rank_portion)
    stacked_b = fetched_b.reshape(blocks_here * rank_portion, -1)
    summed = lax.psum_scatter(
        jnp.dot(head_rows, output_weight, preferred_element_type=jnp.float32)
        + ADAPTER_SCALE * jnp.dot(row_shrink, stacked_b, preferred_element_type=jnp.float32),
        "tensor",
        scatter_dimension=0,
        tiled=True,
    )
    return (hidden.astype(jnp.float32) + summed).astype(jnp.bfloat16)


def solution(mesh):
    in_specs = (
        P(("groups", "store", "tensor"), None),
        P(("groups", "store", "tensor"), None),
        P(("groups", "store", "tensor"), None, None, None),
        P(("groups", "store", "tensor"), None, None, None),
        P(("groups", "store", "tensor")),
        P("tensor", None),
        P(("groups", "store"), None, "tensor"),
        P(("groups", "store"), "tensor", None),
        P(("groups", "store"), None),
        P(("groups", "store")),
        P("groups"),
    )
    out_specs = P(("groups", "store", "tensor"), None)
    return jax.shard_map(
        on_device, mesh=mesh, in_specs=in_specs, out_specs=out_specs, check_vma=False
    )
```

profile of v0, /device:TPU:0, one launch (start us, length us, event | category | flops | bytes accessed | tf_op | source)
XLA Modules:
  0.0 221.9 jit_solution(13661269755926151605)
XLA Ops:
  6.5 0.0 copy-start
  6.5 1.0 copy.21
  7.5 0.7 iota_compare_fusion.2
  8.3 4.4 %fusion.4 = f32[16,8,8,128]{3,2,1,0:T(8,128)S(1)} fusion(bf16[16,8,8,128]{3,2,1,0:T(8,128)(2,1)S(1)} %bitcast.59, bf16[16,8,128,128]{3,2,1,0:T(8,128)(2,1)} %param.13, pred[16,128]{1,0:T(8,128)(4,1)S(1)} %iota_compare_fusion.2), kind=kOutput, calls=%fused_computation.17 | convolution fusion | flops 33816576 | bytes 4982784 | tf_op jit(solution)/shard_map/rkgd,rkpd->rkgp/dot_general | solution.py:12
  12.7 0.0 copy-start.5
  12.7 0.0 copy-start.4
  12.7 0.4 fusion.23
  13.1 4.0 %convolution_convert_fusion = bf16[16,8,8,128]{3,2,1,0:T(8,128)(2,1)S(1)} fusion(bf16[16,8,128,128]{3,2,1,0:T(8,128)(2,1)} %param.14, f32[16,8,8]{2,1,0:T(8,128)S(1)} %fusion.23, f32[16,8,8,128]{3,2,1,0:T(8,128)S(1)} %fusion.4), kind=kOutput, calls=%fused_computation.18 | convolution fusion | flops 34079872 | bytes 4984832 | tf_op jit(solution)/shard_map/rkgp,rkpd->rkgd/dot_general | solution.py:20
  17.1 0.1 all_to_all.20
  17.2 0.9 copy.18
  18.0 6.3 %all-to-all-start = ((bf16[16,4,2048]{2,0,1:T(8,128)(2,1)}), bf16[16,4,2048]{2,0,1:T(8,128)(2,1)S(1)}, u32[]{:S(2)}, u32[]{:S(2)}) async-start(bf16[16,4,2048]{2,0,1:T(8,128)(2,1)} %copy.18), calls=%async_computation | async-start | bytes 524288 | tf_op jit(solution)/shard_map/all_to_all | solution.py:45
  24.3 0.0 copy-done.5
  24.4 0.7 dynamic-slice
  25.7 0.0 copy-done.4
  25.7 0.2 dynamic-update-slice
  26.0 4.9 %all-reduce = s32[32]{0:T(128)S(1)} all-reduce(s32[32]{0:T(128)S(1)} %dynamic-update-slice), channel_id=1, replica_groups=mesh['groups'=2,'store'=4,'tensor'=4] {'store'}, use_global_device_ids=true, to_apply=%add | all-reduce | flops 32 | bytes 256
  30.9 0.0 copy-done
  30.9 0.7 gather_fusion.1
  31.6 0.1 reshape.201
  31.7 0.7 reduce_window_sum.22
  32.5 0.2 fusion.14
  32.6 0.1 select_reduce_fusion
  32.8 0.1 reshape.222
  32.9 6.1 %gather_fusion.2 = bf16[16,64,2048]{2,1,0:T(8,128)(2,1)} fusion(bf16[32,64,2048]{2,1,0:T(8,128)(2,1)} %param.17, s32[1024]{0:T(1024)S(1)} %pad_clamp_fusion.2), kind=kCustom, calls=%fused_computation.2 | custom fusion | bytes 8388672 | tf_op jit(solution)/shard_map/gather | solution.py:66
  39.0 4.5 %broadcast_select_fusion.1 = bf16[4,4,64,2048]{3,2,1,0:T(8,128)(2,1)} fusion(bf16[4,4,64,2048]{3,2,1,0:T(8,128)(2,1)} %bitcast.57, pred[4,4]{1,0:T(4,128)(4,1)S(1)} %fusion.14), kind=kLoop, calls=%fused_computation.13 | loop fusion | flops 2097152 | bytes 8388624 | tf_op jit(solution)/shard_map/jit(_where)/select_n | solution.py:65
  43.5 0.0 all-to-all-done
  43.5 4.9 %all-to-all-start.1 = ((bf16[4,4,64,2048]{3,2,1,0:T(8,128)(2,1)}), bf16[4,4,64,2048]{3,2,1,0:T(8,128)(2,1)}, u32[]{:S(2)}, u32[]{:S(2)}) async-start(bf16[4,4,64,2048]{3,2,1,0:T(8,128)(2,1)} %broadcast_select_fusion.1), calls=%async_computation.1 | async-start | bytes 8388608 | tf_op jit(solution)/shard_map/all_to_all | solution.py:72
  48.4 6.2 %gather_fusion.5 = bf16[16,16,8192]{2,1,0:T(8,128)(2,1)} fusion(bf16[32,16,8192]{2,1,0:T(8,128)(2,1)} %param.18, s32[1024]{0:T(1024)S(1)} %pad_clamp_fusion.2), kind=kCustom, calls=%fused_computation.5 | custom fusion | bytes 8388672 | tf_op jit(solution)/shard_map/gather | solution.py:69
  54.5 4.5 %broadcast_select_fusion = bf16[4,4,16,8192]{3,2,1,0:T(8,128)(2,1)} fusion(bf16[4,4,16,8192]{3,2,1,0:T(8,128)(2,1)} %bitcast.56, pred[4,4]{1,0:T(4,128)(4,1)S(1)} %fusion.14), kind=kLoop, calls=%fused_computation.12 | loop fusion | flops 2097152 | bytes 8388624 | tf_op jit(solution)/shard_map/jit(_where)/select_n | solution.py:68
  59.0 0.0 copy-start.3
  59.0 37.6 %all-to-all-done.1 = bf16[4,4,64,2048]{3,2,1,0:T(8,128)(2,1)} async-done(((bf16[4,4,64,2048]{3,2,1,0:T(8,128)(2,1)}), bf16[4,4,64,2048]{3,2,1,0:T(8,128)(2,1)}, u32[]{:S(2)}, u32[]{:S(2)}) %all-to-all-start.1) | async-done | bytes 4194336 | tf_op jit(solution)/shard_map/all_to_all | solution.py:72
  96.6 4.8 %all-to-all-start.2 = ((bf16[4,4,16,8192]{3,2,1,0:T(8,128)(2,1)}), bf16[4,4,16,8192]{3,2,1,0:T(8,128)(2,1)}, u32[]{:S(2)}, u32[]{:S(2)}) async-start(bf16[4,4,16,8192]{3,2,1,0:T(8,128)(2,1)} %broadcast_select_fusion), calls=%async_computation.2 | async-start | bytes 8388608 | tf_op jit(solution)/shard_map/all_to_all | solution.py:73
  101.5 0.0 reduce-scatter.2.cloned.1.call-start
  101.5 0.6 gather_fusion.3
  102.2 0.2 reduce_window_sum.23
  102.4 0.0 copy-done.3
  102.4 0.1 reshape.206
  102.5 0.1 reshape.260
  102.7 0.9 gather_fusion
  103.6 2.9 %gather_fusion.4 = bf16[8,64,2048]{2,1,0:T(8,128)(2,1)S(1)} fusion(bf16[16,64,2048]{2,1,0:T(8,128)(2,1)} %bitcast.8, s32[1024]{0:T(1024)S(1)} %pad_clamp_fusion), kind=kCustom, calls=%fused_computation.4 | custom fusion | bytes 4194336 | tf_op jit(solution)/shard_map/gather | solution.py:78
  106.5 0.7 fusion.5
  107.2 20.1 %psum.7 = bf16[8,16,64]{2,1,0:T(8,128)(2,1)S(1)} all-reduce(f32[8,16,64]{2,1,0:T(8,128)S(1)} %fusion.5), channel_id=1, replica_groups=mesh['groups'=2,'store'=4,'tensor'=4] {'tensor'}, use_global_device_ids=true, to_apply=%region_8.9 | all-reduce | flops 8192 | bytes 49152 | tf_op jit(solution)/shard_map/psum | solution.py:87
  127.3 0.1 dynamic-slice_convert_fusion
  127.4 6.9 %scatter_fusion = bf16[65,8,16]{2,1,0:T(8,128)(2,1)S(1)} fusion(bf16[65,8,16]{2,1,0:T(8,128)(2,1)S(1)} %broadcast_in_dim.89, s32[128]{0:T(128)S(1)} %reshape.260, bf16[128,16]{1,0:T(8,128)(2,1)S(1)} %bitcast.61), kind=kCustom, calls=%fused_computation.7 | custom fusion | bytes 13312 | tf_op jit(solution)/shard_map/scatter | solution.py:97
  134.4 15.3 %all-to-all-done.2 = bf16[4,4,16,8192]{3,2,1,0:T(8,128)(2,1)} async-done(((bf16[4,4,16,8192]{3,2,1,0:T(8,128)(2,1)}), bf16[4,4,16,8192]{3,2,1,0:T(8,128)(2,1)}, u32[]{:S(2)}, u32[]{:S(2)}) %all-to-all-start.2) | async-done | bytes 4194336 | tf_op jit(solution)/shard_map/all_to_all | solution.py:73
  149.7 2.9 %gather_fusion.6 = bf16[8,16,8192]{2,1,0:T(8,128)(2,1)S(1)} fusion(bf16[16,16,8192]{2,1,0:T(8,128)(2,1)} %bitcast.14, s32[1024]{0:T(1024)S(1)} %pad_clamp_fusion), kind=kCustom, calls=%fused_computation.6 | custom fusion | bytes 4194336 | tf_op jit(solution)/shard_map/gather | solution.py:79
  152.6 0.9 fusion.1
  153.5 0.0 copy-start.2
  153.5 0.0 copy-start.1
  153.5 15.2 %convolution_add_fusion = f32[64,8192]{1,0:T(8,128)} fusion(f32[64,8192]{1,0:T(8,128)S(1)} %fusion.1, bf16[64,2048]{1,0:T(8,128)(2,1)S(1)} %bitcast.55, bf16[2048,8192]{1,0:T(8,128)(2,1)} %param.16), kind=kOutput, calls=%fused_computation.11 | convolution fusion | flops 2148007936 | bytes 38010880 | tf_op jit(solution)/shard_map/dot_general | solution.py:102
  168.7 0.0 reduce-scatter.2.cloned.1.call-update
  168.7 44.6 %reduce-scatter.2.cloned.1.call-done = f32[16,8192]{1,0:T(8,128)} async-done(((f32[64,8192]{1,0:T(8,128)}), f32[16,8192]{1,0:T(8,128)}) %reduce-scatter.2.cloned.1.call-update) | async-done | bytes 524304 | tf_op jit(solution)/shard_map/reduce_scatter | solution.py:101
  213.3 0.0 copy-done.2
  213.3 1.8 add_convert_fusion
  215.1 0.0 copy-done.1
  (22 shorter events, 0.2 us)
Async XLA Ops:
  6.5 24.4 %copy-start = (s32[128]{0:T(128)S(1)}, s32[128]{0:T(128)}, u32[]{:S(2)}) copy-start(s32[128]{0:T(128)} %param.21) | copy-start | bytes 1540
  12.7 11.6 %copy-start.5 = (u32[32]{0:T(128)S(1)}, u32[32]{0:T(128)}, u32[]{:S(2)}) copy-start(u32[32]{0:T(128)} %constant.116) | copy-start | bytes 388
  12.7 13.0 %copy-start.4 = (s32[8]{0:T(128)S(1)}, s32[8]{0:T(128)}, u32[]{:S(2)}) copy-start(s32[8]{0:T(128)} %param.20) | copy-start | bytes 100
  18.0 25.5 %all-to-all-start = ((bf16[16,4,2048]{2,0,1:T(8,128)(2,1)}), bf16[16,4,2048]{2,0,1:T(8,128)(2,1)S(1)}, u32[]{:S(2)}, u32[]{:S(2)}) async-start(bf16[16,4,2048]{2,0,1:T(8,128)(2,1)} %copy.18), calls=%async_computation | async-start | bytes 524288 | tf_op jit(solution)/shard_map/all_to_all | solution.py:45
  43.5 53.1 %all-to-all-start.1 = ((bf16[4,4,64,2048]{3,2,1,0:T(8,128)(2,1)}), bf16[4,4,64,2048]{3,2,1,0:T(8,128)(2,1)}, u32[]{:S(2)}, u32[]{:S(2)}) async-start(bf16[4,4,64,2048]{3,2,1,0:T(8,128)(2,1)} %broadcast_select_fusion.1), calls=%async_computation.1 | async-start | bytes 8388608 | tf_op jit(solution)/shard_map/all_to_all | solution.py:72
  59.0 43.3 %copy-start.3 = (s32[8,16]{1,0:T(8,128)S(1)}, s32[8,16]{1,0:T(8,128)}, u32[]{:S(2)}) copy-start(s32[8,16]{1,0:T(8,128)} %param.19) | copy-start | bytes 1540
  96.6 53.1 %all-to-all-start.2 = ((bf16[4,4,16,8192]{3,2,1,0:T(8,128)(2,1)}), bf16[4,4,16,8192]{3,2,1,0:T(8,128)(2,1)}, u32[]{:S(2)}, u32[]{:S(2)}) async-start(bf16[4,4,16,8192]{3,2,1,0:T(8,128)(2,1)} %broadcast_select_fusion), calls=%async_computation.2 | async-start | bytes 8388608 | tf_op jit(solution)/shard_map/all_to_all | solution.py:73
  101.5 111.8 %reduce-scatter.2.cloned.1.call-start = ((), (), s32[]{:S(2)}) async-start(), calls=%async_computation.4 | async-start | bytes 2621440 | tf_op jit(solution)/shard_map/reduce_scatter | solution.py:101
  153.5 59.8 %copy-start.2 = (bf16[16,8192]{1,0:T(8,128)(2,1)S(1)}, bf16[16,8192]{1,0:T(8,128)(2,1)}, u32[]{:S(2)}) copy-start(bf16[16,8192]{1,0:T(8,128)(2,1)} %param.11) | copy-start | bytes 786436
  153.5 61.6 %copy-start.1 = (s32[128]{0:T(128)S(1)}, s32[128]{0:T(128)}, u32[]{:S(2)}) copy-start(s32[128]{0:T(128)} %param.21) | copy-start | bytes 1540
Sparse Core Ops, SparseCore 0:
  168.8 44.4 reduce-scatter.1
where the time goes:
time: 223 us; the launch traced here: 222 us
  waiting for transfers between devices  97.5 us (44%)
  local copies, waits for them, and re-layouts  30.5 us (14%)
  matrix products  25.2 us (11%)
  blocking collectives  25 us (11%)
  starting transfers between devices  16.1 us (7%)
  between operations  14.3 us (6%)
  other arithmetic  13.3 us (6%)
    reduce_scatter x1, waiting for transfers between devices, on_device(): lax.psum_scatter(jnp.dot(head_rows, output_weight, preferred_element_type...  44.6 us
    all_to_all x1, waiting for transfers between devices, on_device(): lax.all_to_all(outgoing_shrink, 'store', split_axis=0, concat_axis=0, til...  37.6 us
    psum x1, blocking collectives, on_device(): summed_shrink = lax.psum(shrink_part, 'tensor')  20.1 us
    all_to_all x1, waiting for transfers between devices, on_device(): lax.all_to_all(outgoing_expand, 'store', split_axis=0, concat_axis=0, til...  15.3 us
    dot_general x1, matrix products, on_device(): jnp.dot(head_rows, output_weight, preferred_element_type=jnp.float32)  15.2 us
    scatter x1, local copies, waits for them, and re-layouts, on_device(): row_shrink = jnp.zeros((group_rows + 1, blocks_here, rank_portion), jnp.b...  6.94 us
    all_to_all x1, starting transfers between devices, on_device(): lax.all_to_all(attended, 'tensor', split_axis=1, concat_axis=0, tiled=True)  6.32 us
    gather x1, local copies, waits for them, and re-layouts, on_device(): expand_matrices[outgoing_local]  6.16 us
  transfers between devices with their start and end apart: 4, of which 3 were waited for; matrix products, arithmetic and copies ran while one was open for 17% of the time, Pallas kernels for 0%

commit v1 on v0

--- a/solution.py
+++ b/solution.py
@@ -1,9 +1,401 @@
+import functools
+
 import jax
 import jax.numpy as jnp
 from jax import lax
+from jax.experimental import pallas as pl
+from jax.experimental.pallas import tpu as pltpu
 from jax.sharding import PartitionSpec as P
 
 ADAPTER_SCALE = 2.0
+MESH = pl.DeviceIdType.MESH
+CHUNKS = 8
+WEIGHT_SLOTS = 4
+VMEM_BYTES = 60 * 1024 * 1024
+
+
+def attend_kernel(length_ref, q_ref, k_ref, v_ref, out_ref):
+    rows, kv_heads, positions, head_dim = k_ref.shape
+    step = pl.program_id(0)
+    place = lax.broadcasted_iota(jnp.int32, (1, 1, positions), 2)
+    for row in range(rows):
+        q = q_ref[row].reshape(kv_heads, -1, head_dim)
+        scores = lax.dot_general(
+            q, k_ref[row], (((2,), (2,)), ((0,), (0,))), preferred_element_type=jnp.float32
+        ) * head_dim ** (-0.5)
+        scores = jnp.where(place < length_ref[step * rows + row], scores, -jnp.inf)
+        highest = jnp.max(scores, axis=-1, keepdims=True)
+        raised = jnp.exp(scores - highest)
+        weights = (raised / jnp.sum(raised, axis=-1, keepdims=True)).astype(jnp.bfloat16)
+        outputs = lax.dot_general(
+            weights, v_ref[row], (((2,), (1,)), ((0,), (0,))), preferred_element_type=jnp.float32
+        )
+        out_ref[row] = outputs.astype(jnp.bfloat16).reshape(-1, head_dim)
+
+
+def attend_rows(queries, cached_key_rows, cached_value_rows, cache_length):
+    rows_dev, kv_heads, positions, head_dim = cached_key_rows.shape
+    heads = queries.shape[1] // head_dim
+    rows = 2 if rows_dev % 2 == 0 else 1
+    cache_spec = pl.BlockSpec((rows, kv_heads, positions, head_dim), lambda i, n: (i, 0, 0, 0))
+    head_spec = pl.BlockSpec((rows, heads, head_dim), lambda i, n: (i, 0, 0))
+    return pl.pallas_call(
+        attend_kernel,
+        grid_spec=pltpu.PrefetchScalarGridSpec(
+            num_scalar_prefetch=1,
+            grid=(rows_dev // rows,),
+            in_specs=[head_spec, cache_spec, cache_spec],
+            out_specs=head_spec,
+        ),
+        out_shape=jax.ShapeDtypeStruct((rows_dev, heads, head_dim), jnp.bfloat16),
+        compiler_params=pltpu.CompilerParams(vmem_limit_bytes=24 * 1024 * 1024),
+    )(cache_length, queries.reshape(rows_dev, heads, head_dim), cached_key_rows, cached_value_rows)
+
+
+def project_kernel(
+    att_ref,
+    slot_ref,
+    hidden_ref,
+    weight_hbm,
+    shrink_hbm,
+    expand_hbm,
+    out_ref,
+    rows_ref,
+    slots_ref,
+    weight_ref,
+    shrink_ref,
+    expand_ref,
+    base_ref,
+    part_ref,
+    part_recv,
+    mix_ref,
+    delta_ref,
+    near_recv,
+    far_send,
+    far_recv,
+    line_send,
+    line_recv,
+    load_sem,
+    weight_sem,
+    turn_sem,
+    rows_sem,
+    slots_sem,
+    part_sem,
+    near_sem,
+    far_sem,
+    line_sem,
+):
+    store = lax.axis_index("store")
+    tensor = lax.axis_index("tensor")
+    tensors = lax.axis_size("tensor")
+    stores = lax.axis_size("store")
+    near = store + 1 - 2 * (store % 2)
+    far = (store + 2) % 4
+    cross = (near + 2) % 4
+    slots_dev, rank, width = shrink_ref.shape
+    portion = expand_ref.shape[1]
+    rows_dev = att_ref.shape[1]
+    group_rows = tensors * rows_dev
+    rows_all = stores * group_rows
+    chunk = weight_ref.shape[2]
+
+    def line(step):
+        return lax.rem(tensor + step, tensors)
+
+    barrier = pltpu.get_barrier_semaphore()
+    for step in range(1, tensors):
+        pl.semaphore_signal(barrier, inc=1, device_id={"tensor": line(step)}, device_id_type=MESH)
+    for other in (near, far, cross):
+        pl.semaphore_signal(barrier, inc=1, device_id={"store": other}, device_id_type=MESH)
+    shrink_load = pltpu.make_async_copy(shrink_hbm, shrink_ref, load_sem.at[0])
+    expand_load = pltpu.make_async_copy(expand_hbm, expand_ref, load_sem.at[1])
+
+    def weight_load(j):
+        return pltpu.make_async_copy(
+            weight_hbm.at[:, pl.ds(pl.multiple_of(j * chunk, chunk), chunk)],
+            weight_ref.at[lax.rem(j, WEIGHT_SLOTS)],
+            weight_sem.at[lax.rem(j, WEIGHT_SLOTS)],
+        )
+
+    for j in range(2):
+        weight_load(j).start()
+    shrink_load.start()
+    for j in range(2, WEIGHT_SLOTS):
+        weight_load(j).start()
+    expand_load.start()
+    slots_ref[store] = slot_ref[...]
+    pl.semaphore_wait(barrier, tensors - 1 + 3)
+
+    def remote(src, dst, sems, at, **where):
+        return pltpu.make_async_remote_copy(
+            src_ref=src,
+            dst_ref=dst,
+            send_sem=sems.at[(0,) + at],
+            recv_sem=sems.at[(1,) + at],
+            device_id=where,
+            device_id_type=MESH,
+        )
+
+    turns = [
+        remote(att_ref.at[line(step)], rows_ref.at[store, tensor], turn_sem, (step,), tensor=line(step))
+        for step in range(1, tensors)
+    ]
+    for copy in turns:
+        copy.start()
+    rows_ref[store, tensor] = att_ref[tensor]
+
+    slot_copies = [
+        remote(slots_ref.at[store], slots_ref.at[store], slots_sem, (i,), store=other)
+        for i, other in enumerate((near, far, cross))
+    ]
+    for copy in slot_copies:
+        copy.start()
+
+    def share(step):
+        block = rows_ref.at[store, lax.rem(tensor + tensors - step, tensors)]
+        return [
+            remote(block, block, rows_sem, (0, step), store=far),
+            remote(block, block, rows_sem, (1, step), store=near),
+        ]
+
+    shares = [share(step) for step in range(tensors)]
+    for step in range(tensors):
+        if step > 0:
+            turns[step - 1].wait_recv()
+        for copy in shares[step]:
+            copy.start()
+
+    own_rows = rows_ref.at[store]
+
+    def project(j, _):
+        weight_load(j).wait()
+        base_ref[j] = jnp.dot(
+            own_rows[...].reshape(group_rows, width),
+            weight_ref[lax.rem(j, WEIGHT_SLOTS)],
+            preferred_element_type=jnp.float32,
+        )
+        return 0
+
+    relays = []
+    for step in range(tensors):
+        block = rows_ref.at[far, lax.rem(tensor + tensors - step, tensors)]
+        relays.append(remote(block, block, rows_sem, (2, step), store=near))
+
+    lax.fori_loop(0, 2, project, 0)
+    for step in range(tensors):
+        shares[step][0].wait_recv()
+        relays[step].start()
+    lax.fori_loop(2, WEIGHT_SLOTS, project, 0)
+    for j in range(WEIGHT_SLOTS, min(2 * WEIGHT_SLOTS, CHUNKS)):
+        weight_load(j).start()
+    for copy in slot_copies:
+        copy.wait_recv()
+    for step in range(tensors):
+        shares[step][1].wait_recv()
+        relays[step].wait_recv()
+    shrink_load.wait()
+
+    slot_row = jnp.max(jnp.max(slots_ref[...], axis=0), axis=0, keepdims=True) - store * slots_dev
+    batch = 4
+    part_ref[...] = jnp.zeros_like(part_ref)
+
+    def shrink_step(i, _):
+        first = i * batch
+        product = lax.dot_general(
+            shrink_ref[pl.ds(first, batch)].reshape(batch * rank, width),
+            rows_ref[...].reshape(rows_all, width),
+            (((1,), (1,)), ((), ())),
+            preferred_element_type=jnp.float32,
+        ).reshape(batch, rank, rows_all)
+        total = jnp.zeros((rank, rows_all), jnp.float32)
+        for b in range(batch):
+            total += jnp.where(slot_row == first + b, product[b], 0.0)
+        part_ref[...] += total.reshape(part_ref.shape)
+        return 0
+
+    lax.fori_loop(0, slots_dev // batch, shrink_step, 0)
+    parts = [
+        remote(part_ref.at[line(step)], part_recv.at[step - 1], part_sem, (step,), tensor=line(step))
+        for step in range(1, tensors)
+    ]
+    for copy in parts:
+        copy.start()
+    lax.fori_loop(WEIGHT_SLOTS, CHUNKS, project, 0)
+    shrunk = part_ref[tensor]
+    for step in range(1, tensors):
+        parts[step - 1].wait_recv()
+        shrunk += part_recv[step - 1]
+    shrunk = ADAPTER_SCALE * shrunk.astype(jnp.bfloat16).astype(jnp.float32)
+    slot_ids = lax.broadcasted_iota(jnp.int32, (slots_dev, portion, rows_all), 0)
+    spread = jnp.where(slot_row[None] == slot_ids, shrunk[None], 0.0)
+    mix_ref[...] = spread.reshape(slots_dev * portion, rows_all).T.astype(jnp.bfloat16)
+    expand_load.wait()
+
+    def near_copies(j):
+        return [
+            remote(delta_ref.at[j, near], near_recv.at[j, 0], near_sem, (0, j), store=near),
+            remote(delta_ref.at[j, cross], near_recv.at[j, 1], near_sem, (1, j), store=near),
+        ]
+
+    def far_copy(j):
+        return remote(far_send.at[j], far_recv.at[j], far_sem, (j,), store=far)
+
+    def line_copies(j):
+        return [
+            remote(
+                line_send.at[j, line(step)], line_recv.at[j, step - 1], line_sem, (step, j), tensor=line(step)
+            )
+            for step in range(1, tensors)
+        ]
+
+    def columns(j):
+        return pl.ds(pl.multiple_of(j * chunk, chunk), chunk)
+
+    def send_far(j):
+        near_copies(j)[1].wait_recv()
+        total = delta_ref[j, far].astype(jnp.float32) + near_recv[j, 1].astype(jnp.float32)
+        far_send[j] = total.astype(jnp.bfloat16)
+        far_copy(j).start()
+
+    def expand_step(j, _):
+        delta_ref[j] = (
+            jnp.dot(
+                mix_ref[...],
+                expand_ref[:, :, columns(j)].reshape(slots_dev * portion, chunk),
+                preferred_element_type=jnp.float32,
+            )
+            .astype(jnp.bfloat16)
+            .reshape(stores, group_rows, chunk)
+        )
+        for copy in reversed(near_copies(j)):
+            copy.start()
+
+        @pl.when(j > 0)
+        def _():
+            send_far(j - 1)
+
+        return 0
+
+    lax.fori_loop(0, CHUNKS, expand_step, 0)
+    send_far(CHUNKS - 1)
+
+    def line_step(j, _):
+        near_copies(j)[0].wait_recv()
+        far_copy(j).wait_recv()
+        total = (
+            base_ref[j]
+            + delta_ref[j, store].astype(jnp.float32)
+            + near_recv[j, 0].astype(jnp.float32)
+            + far_recv[j].astype(jnp.float32)
+        )
+        line_send[j] = total.astype(jnp.bfloat16).reshape(tensors, rows_dev, chunk)
+        for copy in line_copies(j):
+            copy.start()
+        return 0
+
+    lax.fori_loop(0, CHUNKS, line_step, 0)
+
+    def last_step(j, _):
+        total = hidden_ref[:, columns(j)].astype(jnp.float32) + line_send[j, tensor].astype(jnp.float32)
+        for step, copy in enumerate(line_copies(j)):
+            copy.wait_recv()
+            total += line_recv[j, step].astype(jnp.float32)
+        out_ref[:, columns(j)] = total.astype(jnp.bfloat16)
+        return 0
+
+    lax.fori_loop(0, CHUNKS, last_step, 0)
+
+    for copy in turns + slot_copies + relays + parts:
+        copy.wait_send()
+    for pair in shares:
+        for copy in pair:
+            copy.wait_send()
+
+    def drain(j, _):
+        for copy in near_copies(j) + [far_copy(j)] + line_copies(j):
+            copy.wait_send()
+        return 0
+
+    lax.fori_loop(0, CHUNKS, drain, 0)
+
+
+def rows_plan(
+    hidden,
+    queries,
+    cached_key_rows,
+    cached_value_rows,
+    cache_length,
+    output_weight,
+    shrink_matrices,
+    expand_matrices,
+    block_slot_rows,
+    adapter_per_block,
+    adapter_store_slot,
+):
+    tensors = lax.axis_size("tensor")
+    stores = lax.axis_size("store")
+    rows_dev, model = hidden.shape
+    width = output_weight.shape[0]
+    slots_dev, rank, _ = shrink_matrices.shape
+    portion = expand_matrices.shape[1]
+    group_rows = tensors * rows_dev
+    rows_all = stores * group_rows
+    chunk = model // CHUNKS
+
+    attended = attend_rows(queries, cached_key_rows, cached_value_rows, cache_length)
+    att = attended.reshape(rows_dev, tensors, width).transpose(1, 0, 2)
+
+    slot_of = adapter_store_slot[adapter_per_block]
+    row_ids = jnp.arange(rows_all, dtype=jnp.int32) - lax.axis_index("store") * group_rows
+    listed = block_slot_rows[:, :, None] == row_ids
+    own_slots = jnp.max(jnp.where(listed, slot_of[:, None, None], -1), axis=(0, 1))
+    in_group = (row_ids >= 0) & (row_ids < group_rows)
+    own_slots = jnp.broadcast_to(jnp.where(in_group, own_slots, -1), (8, rows_all))
+
+    vmem = pl.BlockSpec(memory_space=pltpu.VMEM)
+    hbm = pl.BlockSpec(memory_space=pl.ANY)
+    bf16, f32 = jnp.bfloat16, jnp.float32
+    dma = pltpu.SemaphoreType.DMA
+    return pl.pallas_call(
+        project_kernel,
+        out_shape=jax.ShapeDtypeStruct((rows_dev, model), bf16),
+        in_specs=[vmem, vmem, vmem, hbm, hbm, hbm],
+        out_specs=vmem,
+        scratch_shapes=[
+            pltpu.VMEM((stores, tensors, rows_dev, width), bf16),
+            pltpu.VMEM((stores, 8, rows_all), jnp.int32),
+            pltpu.VMEM((WEIGHT_SLOTS, width, chunk), bf16),
+            pltpu.VMEM((slots_dev, rank, width), bf16),
+            pltpu.VMEM((slots_dev, portion, model), bf16),
+            pltpu.VMEM((CHUNKS, group_rows, chunk), f32),
+            pltpu.VMEM((tensors, portion, rows_all), f32),
+            pltpu.VMEM((tensors - 1, portion, rows_all), f32),
+            pltpu.VMEM((rows_all, slots_dev * portion), bf16),
+            pltpu.VMEM((CHUNKS, stores, group_rows, chunk), bf16),
+            pltpu.VMEM((CHUNKS, 2, group_rows, chunk), bf16),
+            pltpu.VMEM((CHUNKS, group_rows, chunk), bf16),
+            pltpu.VMEM((CHUNKS, group_rows, chunk), bf16),
+            pltpu.VMEM((CHUNKS, tensors, rows_dev, chunk), bf16),
+            pltpu.VMEM((CHUNKS, tensors - 1, rows_dev, chunk), bf16),
+            dma((2,)),
+            dma((WEIGHT_SLOTS,)),
+            dma((2, tensors)),
+            dma((2, 3, tensors)),
+            dma((2, 3)),
+            dma((2, tensors)),
+            dma((2, 2, CHUNKS)),
+            dma((2, CHUNKS)),
+            dma((2, tensors, CHUNKS)),
+        ],
+        compiler_params=pltpu.CompilerParams(
+            collective_id=0, has_side_effects=True, vmem_limit_bytes=VMEM_BYTES
+        ),
+        cost_estimate=pl.CostEstimate(
+            flops=2 * model * (group_rows * width + 2 * rows_all * slots_dev * portion),
+            bytes_accessed=2 * (output_weight.size + shrink_matrices.size + expand_matrices.size),
+            transcendentals=0,
+        ),
+    )(att, own_slots, hidden, output_weight, shrink_matrices, expand_matrices)
 
 
 def attend(queries, cached_key_rows, cached_value_rows, cache_length):
@@ -123,6 +515,13 @@
         P("groups"),
     )
     out_specs = P(("groups", "store", "tensor"), None)
+    tensors, stores = mesh.shape["tensor"], mesh.shape["store"]
+
+    def plan(*args):
+        rows_dev, model = args[0].shape
+        fits = stores * tensors * rows_dev * model * 2 <= 4 * 1024 * 1024
+        return (rows_plan if stores == 4 and rows_dev % 16 == 0 and fits else on_device)(*args)
+
     return jax.shard_map(
-        on_device, mesh=mesh, in_specs=in_specs, out_specs=out_specs, check_vma=False
-    )
+        plan, mesh=mesh, in_specs=in_specs, out_specs=out_specs, check_vma=False
+    )

time: 223 us -> 79.4 us (0.36)
  waiting for transfers between devices: 97.5 us -> 0 us
  Pallas kernels: 0 us -> 67.7 us
  matrix products: 25.2 us -> 0 us
  blocking collectives: 25 us -> 0 us
  local copies, waits for them, and re-layouts: 30.5 us -> 9.87 us
  starting transfers between devices: 16.1 us -> 0 us
  between operations: 14.3 us -> 0.06 us
  other arithmetic: 13.3 us -> 1.48 us
    pallas_call x0 -> x2, Pallas kernels: none -> 67.7 us  [the longest x1 59.6 us: rows_plan(): pl.pallas_call(project_kernel, out_shape=jax.ShapeDtypeStruct((rows_dev,...]
    all_to_all x3 -> x0, waiting for transfers between devices: 52.9 us -> none  [the longest x1 37.6 us: on_device(): lax.all_to_all(outgoing_shrink, 'store', split_axis=0, concat_axis=0, til...]
    reduce_scatter x1 -> x0, waiting for transfers between devices: 44.6 us -> none  [on_device(): lax.psum_scatter(jnp.dot(head_rows, output_weight, preferred_element_type...]
    dot_general x5 -> x0, matrix products: 25.2 us -> none  [the longest x1 15.2 us: on_device(): jnp.dot(head_rows, output_weight, preferred_element_type=jnp.float32)]
    psum x1 -> x0, blocking collectives: 20.1 us -> none  [on_device(): summed_shrink = lax.psum(shrink_part, 'tensor')]
    gather x7 -> x1, local copies, waits for them, and re-layouts: 20.3 us -> 0.64 us  [rows_plan(): slot_of = adapter_store_slot[adapter_per_block]]
    all_to_all x3 -> x0, starting transfers between devices: 16 us -> none  [the longest x1 6.32 us: on_device(): lax.all_to_all(attended, 'tensor', split_axis=1, concat_axis=0, tiled=True)]
    select_n x8 -> x2, other arithmetic: 9.06 us -> 0.68 us  [the longest x1 0.67 us: rows_plan(): slot_of = adapter_store_slot[adapter_per_block]]
  transfers between devices with their start and end apart: 4 -> 0, of which waited for: 3 -> 0; matrix products, arithmetic and copies ran while one was open for 17% -> 0% of each run, Pallas kernels for 0% -> 0%
where the time goes in v1:
time: 79.4 us; the launch traced here: 79.1 us
  Pallas kernels  67.7 us (85%)
  local copies, waits for them, and re-layouts  9.87 us (12%)
  other arithmetic  1.48 us (2%)
    pallas_call x1, Pallas kernels, rows_plan(): pl.pallas_call(project_kernel, out_shape=jax.ShapeDtypeStruct((rows_dev,...  59.6 us
    pallas_call x1, Pallas kernels, attend_rows(): pl.pallas_call(attend_kernel, grid_spec=pltpu.PrefetchScalarGridSpec(num_...  8.12 us
    unnamed x10, local copies, waits for them, and re-layouts  7.69 us

profile of v1, /device:TPU:0, one launch (start us, length us, event | category | flops | bytes accessed | tf_op | source)
XLA Modules:
  0.0 79.1 jit_solution(9715429427114133201)
XLA Ops:
  0.0 0.0 copy-start
  0.0 0.7 compare_select_fusion
  0.7 0.0 copy-done
  0.7 0.6 gather_fusion
  1.3 0.8 %select_reduce_fusion = s32[256]{0:T(256)S(1)} fusion(s32[8]{0:T(128)S(1)} %gather_fusion, s32[256]{0:T(256)S(1)} %iota_subtract_fusion, s32[8,16]{1,0:T(8,128)} %param.19), kind=kLoop, calls=%fused_computation.2 | loop fusion | flops 98048 | bytes 2592 | tf_op jit(solution)/shard_map/reduce_max | solution.py:351
  2.2 0.6 broadcast_in_dim.29.slot_ref
  2.8 1.0 %copy.14 = bf16[2,8,64,128]{3,2,1,0:T(8,128)(2,1)S(1)} copy(bf16[2,8,64,128]{3,1,2,0:T(8,128)(2,1)} %bitcast.7) | data formatting | bytes 524288
  3.8 0.0 copy-start.1
  3.8 2.2 %copy-done.1 = bf16[16,8,128,128]{3,2,1,0:T(8,128)(2,1)S(1)} copy-done((bf16[16,8,128,128]{3,2,1,0:T(8,128)(2,1)S(1)}, bf16[16,8,128,128]{3,2,1,0:T(8,128)(2,1)}, u32[]{:S(2)}) %copy-start.1) | copy-done | bytes 4194328
  5.9 0.0 copy-start.2
  6.0 2.2 %copy-done.2 = bf16[16,8,128,128]{3,2,1,0:T(8,128)(2,1)S(1)} copy-done((bf16[16,8,128,128]{3,2,1,0:T(8,128)(2,1)S(1)}, bf16[16,8,128,128]{3,2,1,0:T(8,128)(2,1)}, u32[]{:S(2)}) %copy-start.2) | copy-done | bytes 4194328
  8.1 0.0 copy-start.3
  8.1 0.7 copy-done.3
  8.8 8.1 %shard_map.109 = bf16[16,64,128]{2,1,0:T(8,128)(2,1)S(1)} custom-call(s32[16]{0:T(128)S(1)} %copy-done.3, bf16[16,64,128]{2,1,0:T(8,128)(2,1)S(1)} %bitcast.5, bf16[16,8,128,128]{3,2,1,0:T(8,128)(2,1)S(1)} %copy-done.1, bf16[16,8,128,128]{3,2,1,0:T(8,128)(2,1)S(1)} %copy-done.2), custom_call_target="tpu_custom_call" | custom-call | tf_op jit(solution)/shard_map/pallas_call | solution.py:42
  16.9 0.1 reshape.13
  17.0 0.9 %copy.16 = bf16[16,4,2048]{2,0,1:T(8,128)(2,1)} copy(bf16[16,4,2048]{2,1,0:T(4,128)(2,1)S(1)} %reshape.13) | data formatting | bytes 524288 | tf_op jit(solution)/shard_map/reshape | solution.py:346
  17.9 59.6 %shard_map.110 = bf16[16,8192]{1,0:T(8,128)(2,1)} custom-call(bf16[4,16,2048]{2,1,0:T(8,128)(2,1)} %bitcast.6, s32[8,256]{1,0:T(8,128)} %broadcast_in_dim.29.slot_ref, bf16[16,8192]{1,0:T(8,128)(2,1)} %hidden_ref.1, bf16[2048,8192]{1,0:T(8,128)(2,1)} %weight_hbm.1, bf16[32,64,2048]{2,1,0:T(8,128)(2,1)} %shrink_hbm.1, bf16[32,16,8192]{2,1,0:T(8,128)(2,1)} %expand_hbm.1), custom_call_target="tpu_custom_call" | custom-call | flops 6442450944 | bytes 50331648 | tf_op jit(solution)/shard_map/pallas_call | solution.py:359
  77.5 1.7 %copy.18 = bf16[16,8192]{1,0:T(8,128)(2,1)} copy(bf16[16,8192]{1,0:T(8,128)(2,1)} %shard_map.110) | data formatting | bytes 524288
  (3 shorter events, 0.0 us)
Async XLA Ops:
  0.0 0.7 copy-start
  3.8 2.2 %copy-start.1 = (bf16[16,8,128,128]{3,2,1,0:T(8,128)(2,1)S(1)}, bf16[16,8,128,128]{3,2,1,0:T(8,128)(2,1)}, u32[]{:S(2)}) copy-start(bf16[16,8,128,128]{3,2,1,0:T(8,128)(2,1)} %k_ref.1) | copy-start | bytes 12582916
  5.9 2.2 %copy-start.2 = (bf16[16,8,128,128]{3,2,1,0:T(8,128)(2,1)S(1)}, bf16[16,8,128,128]{3,2,1,0:T(8,128)(2,1)}, u32[]{:S(2)}) copy-start(bf16[16,8,128,128]{3,2,1,0:T(8,128)(2,1)} %v_ref.1) | copy-start | bytes 12582916
  8.1 0.7 copy-start.3

commit v2 on v1

--- a/solution.py
+++ b/solution.py
@@ -14,52 +14,24 @@
 VMEM_BYTES = 60 * 1024 * 1024
 
 
-def attend_kernel(length_ref, q_ref, k_ref, v_ref, out_ref):
-    rows, kv_heads, positions, head_dim = k_ref.shape
-    step = pl.program_id(0)
-    place = lax.broadcasted_iota(jnp.int32, (1, 1, positions), 2)
-    for row in range(rows):
-        q = q_ref[row].reshape(kv_heads, -1, head_dim)
-        scores = lax.dot_general(
-            q, k_ref[row], (((2,), (2,)), ((0,), (0,))), preferred_element_type=jnp.float32
-        ) * head_dim ** (-0.5)
-        scores = jnp.where(place < length_ref[step * rows + row], scores, -jnp.inf)
-        highest = jnp.max(scores, axis=-1, keepdims=True)
-        raised = jnp.exp(scores - highest)
-        weights = (raised / jnp.sum(raised, axis=-1, keepdims=True)).astype(jnp.bfloat16)
-        outputs = lax.dot_general(
-            weights, v_ref[row], (((2,), (1,)), ((0,), (0,))), preferred_element_type=jnp.float32
-        )
-        out_ref[row] = outputs.astype(jnp.bfloat16).reshape(-1, head_dim)
-
-
-def attend_rows(queries, cached_key_rows, cached_value_rows, cache_length):
-    rows_dev, kv_heads, positions, head_dim = cached_key_rows.shape
-    heads = queries.shape[1] // head_dim
-    rows = 2 if rows_dev % 2 == 0 else 1
-    cache_spec = pl.BlockSpec((rows, kv_heads, positions, head_dim), lambda i, n: (i, 0, 0, 0))
-    head_spec = pl.BlockSpec((rows, heads, head_dim), lambda i, n: (i, 0, 0))
-    return pl.pallas_call(
-        attend_kernel,
-        grid_spec=pltpu.PrefetchScalarGridSpec(
-            num_scalar_prefetch=1,
-            grid=(rows_dev // rows,),
-            in_specs=[head_spec, cache_spec, cache_spec],
-            out_specs=head_spec,
-        ),
-        out_shape=jax.ShapeDtypeStruct((rows_dev, heads, head_dim), jnp.bfloat16),
-        compiler_params=pltpu.CompilerParams(vmem_limit_bytes=24 * 1024 * 1024),
-    )(cache_length, queries.reshape(rows_dev, heads, head_dim), cached_key_rows, cached_value_rows)
-
-
 def project_kernel(
-    att_ref,
-    slot_ref,
+    length_ref,
+    adapter_ref,
+    table_ref,
+    listed_ref,
     hidden_ref,
+    q_ref,
+    key_hbm,
+    value_hbm,
     weight_hbm,
     shrink_hbm,
     expand_hbm,
     out_ref,
+    key_ref,
+    value_ref,
+    live_ref,
+    heads_ref,
+    att_ref,
     rows_ref,
     slots_ref,
     weight_ref,
@@ -76,6 +48,7 @@
     line_send,
     line_recv,
     load_sem,
+    cache_sem,
     weight_sem,
     turn_sem,
     rows_sem,
@@ -95,6 +68,8 @@
     slots_dev, rank, width = shrink_ref.shape
     portion = expand_ref.shape[1]
     rows_dev = att_ref.shape[1]
+    _, _, kv_heads, positions, head_dim = key_ref.shape
+    heads = width // head_dim
     group_rows = tensors * rows_dev
     rows_all = stores * group_rows
     chunk = weight_ref.shape[2]
@@ -117,13 +92,37 @@
             weight_sem.at[lax.rem(j, WEIGHT_SLOTS)],
         )
 
+    def cache_loads(i):
+        heads_of = pl.ds(line(lax.rem(i + 1, tensors)) * kv_heads, kv_heads)
+        return [
+            pltpu.make_async_copy(key_hbm.at[:, heads_of], key_ref.at[i], cache_sem.at[0, i]),
+            pltpu.make_async_copy(value_hbm.at[:, heads_of], value_ref.at[i], cache_sem.at[1, i]),
+        ]
+
+    for i in range(tensors):
+        for copy in cache_loads(i):
+            copy.start()
     for j in range(2):
         weight_load(j).start()
     shrink_load.start()
     for j in range(2, WEIGHT_SLOTS):
         weight_load(j).start()
     expand_load.start()
-    slots_ref[store] = slot_ref[...]
+
+    blocks, block_slots = listed_ref.shape
+    row_ids = lax.broadcasted_iota(jnp.int32, (blocks, rows_all), 1) - store * group_rows
+    block_ids = lax.broadcasted_iota(jnp.int32, (blocks, rows_all), 0)
+    block_slot = jnp.zeros((blocks, rows_all), jnp.int32)
+    for b in range(blocks):
+        block_slot = jnp.where(block_ids == b, table_ref[adapter_ref[b]], block_slot)
+    own_slots = jnp.full((blocks, rows_all), -1, jnp.int32)
+    for i in range(block_slots):
+        named = (listed_ref[:, i : i + 1] == row_ids) & (row_ids >= 0)
+        own_slots = jnp.where(named, block_slot, own_slots)
+    slots_ref[store] = own_slots
+    places = lax.broadcasted_iota(jnp.int32, live_ref.shape[1:], 1)
+    for row in range(rows_dev):
+        live_ref[row] = jnp.where(places < length_ref[row], 1, 0)
     pl.semaphore_wait(barrier, tensors - 1 + 3)
 
     def remote(src, dst, sems, at, **where):
@@ -136,14 +135,6 @@
             device_id_type=MESH,
         )
 
-    turns = [
-        remote(att_ref.at[line(step)], rows_ref.at[store, tensor], turn_sem, (step,), tensor=line(step))
-        for step in range(1, tensors)
-    ]
-    for copy in turns:
-        copy.start()
-    rows_ref[store, tensor] = att_ref[tensor]
-
     slot_copies = [
         remote(slots_ref.at[store], slots_ref.at[store], slots_sem, (i,), store=other)
         for i, other in enumerate((near, far, cross))
@@ -151,6 +142,11 @@
     for copy in slot_copies:
         copy.start()
 
+    def turn(step):
+        return remote(
+            att_ref.at[line(step)], rows_ref.at[store, tensor], turn_sem, (step,), tensor=line(step)
+        )
+
     def share(step):
         block = rows_ref.at[store, lax.rem(tensor + tensors - step, tensors)]
         return [
@@ -158,12 +154,62 @@
             remote(block, block, rows_sem, (1, step), store=near),
         ]
 
+    def attend(i):
+        target = line(lax.rem(i + 1, tensors))
+        for head in range(heads):
+            first = pl.multiple_of(target * width + head * head_dim, head_dim)
+            heads_ref[pl.ds(head, rows_dev, stride=heads), :] = q_ref[
+                :, pl.ds(first, head_dim)
+            ].astype(jnp.float32)
+        for copy in cache_loads(i):
+            copy.wait()
+        q = heads_ref[...].astype(jnp.bfloat16).reshape(rows_dev * kv_heads, -1, head_dim)
+        scores = lax.dot_general(
+            q,
+            key_ref[i].reshape(rows_dev * kv_heads, positions, head_dim),
+            (((2,), (2,)), ((0,), (0,))),
+            preferred_element_type=jnp.float32,
+        ) * head_dim ** (-0.5)
+        live = (live_ref[...] > 0)[:, None]
+        scores = scores.reshape((rows_dev, kv_heads) + scores.shape[1:])
+        scores = jnp.where(live, scores, -jnp.inf)
+        highest = jnp.max(scores, axis=-1, keepdims=True)
+        raised = jnp.exp(scores - highest)
+        weights = (raised / jnp.sum(raised, axis=-1, keepdims=True)).astype(jnp.bfloat16)
+        outputs = lax.dot_general(
+            weights.reshape(rows_dev * kv_heads, -1, positions),
+            value_ref[i].reshape(rows_dev * kv_heads, positions, head_dim),
+            (((2,), (1,)), ((0,), (0,))),
+            preferred_element_type=jnp.float32,
+        )
+        heads_ref[...] = outputs.reshape(rows_dev * heads, head_dim)
+        for head in range(heads):
+            att_ref[target, :, head * head_dim : (head + 1) * head_dim] = heads_ref[
+                pl.ds(head, rows_dev, stride=heads), :
+            ].astype(jnp.bfloat16)
+
+    def attend_step(i, _):
+        attend(i)
+        turn(i + 1).start()
+
+        @pl.when(i > 0)
+        def _():
+            turn(i).wait_recv()
+            for copy in share(i):
+                copy.start()
+
+        return 0
+
+    lax.fori_loop(0, tensors - 1, attend_step, 0)
+    attend(tensors - 1)
+    rows_ref[store, tensor] = att_ref[tensor]
+    for copy in share(0):
+        copy.start()
+    turn(tensors - 1).wait_recv()
+    for copy in share(tensors - 1):
+        copy.start()
+    turns = [turn(step) for step in range(1, tensors)]
     shares = [share(step) for step in range(tensors)]
-    for step in range(tensors):
-        if step > 0:
-            turns[step - 1].wait_recv()
-        for copy in shares[step]:
-            copy.start()
 
     own_rows = rows_ref.at[store]
 
@@ -220,7 +266,7 @@
     ]
     for copy in parts:
         copy.start()
-    lax.fori_loop(WEIGHT_SLOTS, CHUNKS, project, 0)
+    lax.fori_loop(WEIGHT_SLOTS, CHUNKS - 2, project, 0)
     shrunk = part_ref[tensor]
     for step in range(1, tensors):
         parts[step - 1].wait_recv()
@@ -278,6 +324,7 @@
 
     lax.fori_loop(0, CHUNKS, expand_step, 0)
     send_far(CHUNKS - 1)
+    lax.fori_loop(CHUNKS - 2, CHUNKS, project, 0)
 
     def line_step(j, _):
         near_copies(j)[0].wait_recv()
@@ -342,26 +389,26 @@
     rows_all = stores * group_rows
     chunk = model // CHUNKS
 
-    attended = attend_rows(queries, cached_key_rows, cached_value_rows, cache_length)
-    att = attended.reshape(rows_dev, tensors, width).transpose(1, 0, 2)
-
-    slot_of = adapter_store_slot[adapter_per_block]
-    row_ids = jnp.arange(rows_all, dtype=jnp.int32) - lax.axis_index("store") * group_rows
-    listed = block_slot_rows[:, :, None] == row_ids
-    own_slots = jnp.max(jnp.where(listed, slot_of[:, None, None], -1), axis=(0, 1))
-    in_group = (row_ids >= 0) & (row_ids < group_rows)
-    own_slots = jnp.broadcast_to(jnp.where(in_group, own_slots, -1), (8, rows_all))
+    kv_heads, positions, head_dim = cached_key_rows.shape[1:]
+    heads = width // head_dim
+    kv_part = kv_heads // tensors
 
     vmem = pl.BlockSpec(memory_space=pltpu.VMEM)
+    smem = pl.BlockSpec(memory_space=pltpu.SMEM)
     hbm = pl.BlockSpec(memory_space=pl.ANY)
     bf16, f32 = jnp.bfloat16, jnp.float32
     dma = pltpu.SemaphoreType.DMA
     return pl.pallas_call(
         project_kernel,
         out_shape=jax.ShapeDtypeStruct((rows_dev, model), bf16),
-        in_specs=[vmem, vmem, vmem, hbm, hbm, hbm],
+        in_specs=[smem, smem, smem, vmem, vmem, vmem, hbm, hbm, hbm, hbm, hbm],
         out_specs=vmem,
         scratch_shapes=[
+            pltpu.VMEM((tensors, rows_dev, kv_part, positions, head_dim), bf16),
+            pltpu.VMEM((tensors, rows_dev, kv_part, positions, head_dim), bf16),
+            pltpu.VMEM((rows_dev, heads // kv_part, positions), jnp.int32),
+            pltpu.VMEM((rows_dev * heads, head_dim), f32),
+            pltpu.VMEM((tensors, rows_dev, width), bf16),
             pltpu.VMEM((stores, tensors, rows_dev, width), bf16),
             pltpu.VMEM((stores, 8, rows_all), jnp.int32),
             pltpu.VMEM((WEIGHT_SLOTS, width, chunk), bf16),
@@ -378,6 +425,7 @@
             pltpu.VMEM((CHUNKS, tensors, rows_dev, chunk), bf16),
             pltpu.VMEM((CHUNKS, tensors - 1, rows_dev, chunk), bf16),
             dma((2,)),
+            dma((2, tensors)),
             dma((WEIGHT_SLOTS,)),
             dma((2, tensors)),
             dma((2, 3, tensors)),
@@ -395,7 +443,19 @@
             bytes_accessed=2 * (output_weight.size + shrink_matrices.size + expand_matrices.size),
             transcendentals=0,
         ),
-    )(att, own_slots, hidden, output_weight, shrink_matrices, expand_matrices)
+    )(
+        cache_length,
+        adapter_per_block,
+        adapter_store_slot,
+        block_slot_rows,
+        hidden,
+        queries,
+        cached_key_rows,
+        cached_value_rows,
+        output_weight,
+        shrink_matrices,
+        expand_matrices,
+    )
 
 
 def attend(queries, cached_key_rows, cached_value_rows, cache_length):
@@ -519,8 +579,10 @@
 
     def plan(*args):
         rows_dev, model = args[0].shape
+        kv_heads = args[2].shape[1]
         fits = stores * tensors * rows_dev * model * 2 <= 4 * 1024 * 1024
-        return (rows_plan if stores == 4 and rows_dev % 16 == 0 and fits else on_device)(*args)
+        fits = fits and stores == 4 and rows_dev % 16 == 0 and kv_heads % tensors == 0
+        return (rows_plan if fits else on_device)(*args)
 
     return jax.shard_map(
         plan, mesh=mesh, in_specs=in_specs, out_specs=out_specs, check_vma=False

time: 79.4 us -> 66.5 us (0.84)
  local copies, waits for them, and re-layouts: 9.87 us -> 1.67 us
  Pallas kernels: 67.7 us -> 64.6 us
  other arithmetic: 1.48 us -> 0 us
    pallas_call x1 -> x0, Pallas kernels: 8.12 us -> none  [attend_rows(): pl.pallas_call(attend_kernel, grid_spec=pltpu.PrefetchScalarGridSpec(num_...]
    unnamed x10 -> x1, local copies, waits for them, and re-layouts: 7.69 us -> 1.67 us
    pallas_call x1, Pallas kernels: 59.6 us -> 64.6 us  [rows_plan(): pl.pallas_call(project_kernel, out_shape=jax.ShapeDtypeStruct((rows_dev,...]
    reshape x2 -> x0, local copies, waits for them, and re-layouts: 0.93 us -> none  [rows_plan(): att = attended.reshape(rows_dev, tensors, width).transpose(1, 0, 2)]
    reduce_max x1 -> x0, other arithmetic: 0.8 us -> none  [rows_plan(): jnp.max(jnp.where(listed, slot_of[:, None, None], -1), axis=(0, 1))]
where the time goes in v2:
time: 66.5 us; the launch traced here: 66.3 us
  Pallas kernels  64.6 us (97%)
  local copies, waits for them, and re-layouts  1.67 us (3%)
    pallas_call x1, Pallas kernels, rows_plan(): pl.pallas_call(project_kernel, out_shape=jax.ShapeDtypeStruct((rows_dev,...  64.6 us
    unnamed x1, local copies, waits for them, and re-layouts  1.67 us

profile of v2, /device:TPU:0, one launch (start us, length us, event | category | flops | bytes accessed | tf_op | source)
XLA Modules:
  0.0 66.3 jit_solution(11087541415047592386)
XLA Ops:
  0.0 64.6 %shard_map.109 = bf16[16,8192]{1,0:T(8,128)(2,1)} custom-call(s32[16]{0:T(128)} %length_ref.1, s32[8]{0:T(128)} %adapter_ref.1, s32[128]{0:T(128)} %table_ref.1, s32[8,16]{1,0:T(8,128)} %listed_ref.1, bf16[16,8192]{1,0:T(8,128)(2,1)} %hidden_ref.1, bf16[16,8192]{1,0:T(8,128)(2,1)} %q_ref.1, bf16[16,8,128,128]{3,2,1,0:T(8,128)(2,1)} %key_hbm.1, ...), custom_call_target="tpu_custom_call" | custom-call | flops 6442450944 | bytes 50331648 | tf_op jit(solution)/shard_map/pallas_call | solution.py:401
  64.6 1.7 %copy.13 = bf16[16,8192]{1,0:T(8,128)(2,1)} copy(bf16[16,8192]{1,0:T(8,128)(2,1)} %shard_map.109) | data formatting | bytes 524288

commit v3 on v2

--- a/solution.py
+++ b/solution.py
@@ -11,6 +11,8 @@
 MESH = pl.DeviceIdType.MESH
 CHUNKS = 8
 WEIGHT_SLOTS = 4
+FIRST = 4
+EARLY = 8
 VMEM_BYTES = 60 * 1024 * 1024
 
 
@@ -93,7 +95,7 @@
         )
 
     def cache_loads(i):
-        heads_of = pl.ds(line(lax.rem(i + 1, tensors)) * kv_heads, kv_heads)
+        heads_of = pl.ds(line(i) * kv_heads, kv_heads)
         return [
             pltpu.make_async_copy(key_hbm.at[:, heads_of], key_ref.at[i], cache_sem.at[0, i]),
             pltpu.make_async_copy(value_hbm.at[:, heads_of], value_ref.at[i], cache_sem.at[1, i]),
@@ -102,13 +104,6 @@
     for i in range(tensors):
         for copy in cache_loads(i):
             copy.start()
-    for j in range(2):
-        weight_load(j).start()
-    shrink_load.start()
-    for j in range(2, WEIGHT_SLOTS):
-        weight_load(j).start()
-    expand_load.start()
-
     blocks, block_slots = listed_ref.shape
     row_ids = lax.broadcasted_iota(jnp.int32, (blocks, rows_all), 1) - store * group_rows
     block_ids = lax.broadcasted_iota(jnp.int32, (blocks, rows_all), 0)
@@ -123,7 +118,6 @@
     places = lax.broadcasted_iota(jnp.int32, live_ref.shape[1:], 1)
     for row in range(rows_dev):
         live_ref[row] = jnp.where(places < length_ref[row], 1, 0)
-    pl.semaphore_wait(barrier, tensors - 1 + 3)
 
     def remote(src, dst, sems, at, **where):
         return pltpu.make_async_remote_copy(
@@ -135,13 +129,6 @@
             device_id_type=MESH,
         )
 
-    slot_copies = [
-        remote(slots_ref.at[store], slots_ref.at[store], slots_sem, (i,), store=other)
-        for i, other in enumerate((near, far, cross))
-    ]
-    for copy in slot_copies:
-        copy.start()
-
     def turn(step):
         return remote(
             att_ref.at[line(step)], rows_ref.at[store, tensor], turn_sem, (step,), tensor=line(step)
@@ -154,8 +141,22 @@
             remote(block, block, rows_sem, (1, step), store=near),
         ]
 
+    def follow(i):
+        @pl.when(i == 0)
+        def _():
+            shrink_load.start()
+
+        @pl.when(i == 1)
+        def _():
+            expand_load.start()
+
+        @pl.when(i == 2)
+        def _():
+            for j in range(WEIGHT_SLOTS):
+                weight_load(j).start()
+
     def attend(i):
-        target = line(lax.rem(i + 1, tensors))
+        target = line(i)
         for head in range(heads):
             first = pl.multiple_of(target * width + head * head_dim, head_dim)
             heads_ref[pl.ds(head, rows_dev, stride=heads), :] = q_ref[
@@ -163,6 +164,7 @@
             ].astype(jnp.float32)
         for copy in cache_loads(i):
             copy.wait()
+        follow(i)
         q = heads_ref[...].astype(jnp.bfloat16).reshape(rows_dev * kv_heads, -1, head_dim)
         scores = lax.dot_general(
             q,
@@ -190,23 +192,30 @@
 
     def attend_step(i, _):
         attend(i)
-        turn(i + 1).start()
-
-        @pl.when(i > 0)
+        turn(i).start()
+
+        @pl.when(i > 1)
         def _():
-            turn(i).wait_recv()
-            for copy in share(i):
+            turn(i - 1).wait_recv()
+            for copy in share(i - 1):
                 copy.start()
 
         return 0
 
-    lax.fori_loop(0, tensors - 1, attend_step, 0)
-    attend(tensors - 1)
+    attend(0)
     rows_ref[store, tensor] = att_ref[tensor]
+    pl.semaphore_wait(barrier, tensors - 1 + 3)
     for copy in share(0):
         copy.start()
+    lax.fori_loop(1, tensors, attend_step, 0)
     turn(tensors - 1).wait_recv()
     for copy in share(tensors - 1):
+        copy.start()
+    slot_copies = [
+        remote(slots_ref.at[store], slots_ref.at[store], slots_sem, (i,), store=other)
+        for i, other in enumerate((near, far, cross))
+    ]
+    for copy in slot_copies:
         copy.start()
     turns = [turn(step) for step in range(1, tensors)]
     shares = [share(step) for step in range(tensors)]
@@ -220,6 +229,11 @@
             weight_ref[lax.rem(j, WEIGHT_SLOTS)],
             preferred_element_type=jnp.float32,
         )
+
+        @pl.when(j + WEIGHT_SLOTS < CHUNKS)
+        def _():
+            weight_load(j + WEIGHT_SLOTS).start()
+
         return 0
 
     relays = []
@@ -227,13 +241,10 @@
         block = rows_ref.at[far, lax.rem(tensor + tensors - step, tensors)]
         relays.append(remote(block, block, rows_sem, (2, step), store=near))
 
-    lax.fori_loop(0, 2, project, 0)
+    lax.fori_loop(0, FIRST, project, 0)
     for step in range(tensors):
         shares[step][0].wait_recv()
         relays[step].start()
-    lax.fori_loop(2, WEIGHT_SLOTS, project, 0)
-    for j in range(WEIGHT_SLOTS, min(2 * WEIGHT_SLOTS, CHUNKS)):
-        weight_load(j).start()
     for copy in slot_copies:
         copy.wait_recv()
     for step in range(tensors):
@@ -266,7 +277,7 @@
     ]
     for copy in parts:
         copy.start()
-    lax.fori_loop(WEIGHT_SLOTS, CHUNKS - 2, project, 0)
+    lax.fori_loop(FIRST, EARLY, project, 0)
     shrunk = part_ref[tensor]
     for step in range(1, tensors):
         parts[step - 1].wait_recv()
@@ -324,7 +335,6 @@
 
     lax.fori_loop(0, CHUNKS, expand_step, 0)
     send_far(CHUNKS - 1)
-    lax.fori_loop(CHUNKS - 2, CHUNKS, project, 0)
 
     def line_step(j, _):
         near_copies(j)[0].wait_recv()

time: 66.5 us -> 64.3 us (0.967)
  Pallas kernels: 64.6 us -> 62.5 us
    pallas_call x1, Pallas kernels: 64.6 us -> 62.5 us  [rows_plan(): pl.pallas_call(project_kernel, out_shape=jax.ShapeDtypeStruct((rows_dev,...]
where the time goes in v3:
time: 64.3 us; the launch traced here: 64.1 us
  Pallas kernels  62.5 us (97%)
  local copies, waits for them, and re-layouts  1.67 us (3%)
    pallas_call x1, Pallas kernels, rows_plan(): pl.pallas_call(project_kernel, out_shape=jax.ShapeDtypeStruct((rows_dev,...  62.5 us
    unnamed x1, local copies, waits for them, and re-layouts  1.67 us

profile of v3, /device:TPU:0, one launch (start us, length us, event | category | flops | bytes accessed | tf_op | source)
XLA Modules:
  0.0 64.1 jit_solution(14803697659074870924)
XLA Ops:
  0.0 62.5 %shard_map.109 = bf16[16,8192]{1,0:T(8,128)(2,1)} custom-call(s32[16]{0:T(128)} %length_ref.1, s32[8]{0:T(128)} %adapter_ref.1, s32[128]{0:T(128)} %table_ref.1, s32[8,16]{1,0:T(8,128)} %listed_ref.1, bf16[16,8192]{1,0:T(8,128)(2,1)} %hidden_ref.1, bf16[16,8192]{1,0:T(8,128)(2,1)} %q_ref.1, bf16[16,8,128,128]{3,2,1,0:T(8,128)(2,1)} %key_hbm.1, ...), custom_call_target="tpu_custom_call" | custom-call | flops 6442450944 | bytes 50331648 | tf_op jit(solution)/shard_map/pallas_call | solution.py:411
  62.5 1.7 %copy.13 = bf16[16,8192]{1,0:T(8,128)(2,1)} copy(bf16[16,8192]{1,0:T(8,128)(2,1)} %shard_map.109) | data formatting | bytes 524288
